TPU v7x, 768 devices: a whole 4x8x12 slice. The times are simulated.
768 devices in a mesh: rep: 8 (over y), seq: 24 (over z, core), fsdp: 4 (over x).
Axes of the slice: x: 4, y: 8, z: 12, core: 2. Of those that a mesh axis runs over, the one named last changes fastest.
Arguments:
- tokens: bfloat16 [49152, 4096], P(('rep', 'seq')), may hold values from -6 to 6
- cotangent: bfloat16 [49152, 4096], P(('rep', 'seq')), may hold values from -3 to 3
- norm_gain: float32 [4096], replicated, may hold values from 0.1 to 1.9
- gate_weight: bfloat16 [4096, 12288], P(None, ('seq', 'fsdp')), may hold values from -0.09375 to 0.09375
- up_weight: bfloat16 [4096, 12288], P(None, ('seq', 'fsdp')), may hold values from -0.09375 to 0.09375
- down_weight: bfloat16 [12288, 4096], P(('seq', 'fsdp')), may hold values from -0.0546875 to 0.0546875
- depths: int32 [49152], P(('rep', 'seq')), may hold values from 0 to 4, as said below
Outputs:
- branch_grad: bfloat16 [49152, 4096], P(('rep', 'seq', 'fsdp'))
- gate_grad: float32 [4096, 12288], P('rep', ('seq', 'fsdp'))
- up_grad: float32 [4096, 12288], P('rep', ('seq', 'fsdp'))
- down_grad: float32 [12288, 4096], P(('seq', 'fsdp'), 'rep')
Inputs may be any that keep to these rules, and one draw needn't show every extreme that they name: `depths`: within each aligned block of 256 rows (the tokens of one seq shard) at most 8 and at least 4 tokens have a depth greater than 1, and some block has exactly 8.
All inputs are finite; a program needn't handle non-finite values.
Results may differ from a plain program's by a relative error of at most 0.019.
Values may be sent and summed in bfloat16 or wider, within the bound.
A program may use at most 64 MiB of HBM per device.

v0:
```python
from functools import partial

import jax
import jax.numpy as jnp
from jax import lax
from jax.sharding import Mesh
from jax.sharding import PartitionSpec as P

REC = 1
MAXACT = 8
SEQ = ("seq_0", "seq_1")
REP_SEQ = ("rep", "seq_0", "seq_1")
SEQ_FSDP = ("seq_0", "seq_1", "fsdp")
REP_SEQ_FSDP = ("rep", "seq_0", "seq_1", "fsdp")


EPSILON = 1e-05


def side_by_side(arrays, axis, dim, along):
    ends, at = ([], 0)
    for a in arrays[:-1]:
        at += a.shape[along]
        ends.append(at)
    both = jnp.concatenate(arrays, axis=along)
    return tuple(jnp.split(lax.all_gather(both, axis, axis=dim, tiled=True), ends, axis=along))


def in_blocks(x, dim, size):
    lengths = x.shape
    tiles = x.reshape(*lengths[:dim], size, lengths[dim] // size, *lengths[dim + 1 :])
    return jnp.moveaxis(tiles, dim, 0)


def sum_together(arrays, axis, dims):
    size = lax.axis_size(axis)
    tiles = [in_blocks(a, dim, size) for a, dim in zip(arrays, dims)]
    lines = jnp.concatenate([b.reshape(size, -1) for b in tiles], axis=1)
    width = max(16, -(-lines.shape[1] // 1024) * 8)
    lines = jnp.pad(lines, ((0, 0), (0, width * 128 - lines.shape[1]))).reshape(-1, 128)
    line, at, finished = (lax.psum_scatter(lines, axis, tiled=True).reshape(-1), 0, [])
    for b in tiles:
        part = b[0]
        finished.append(line[at : at + part.size].reshape(part.shape))
        at += part.size
    return tuple(finished)


def reduced_to_own(tiles, axes, turns):
    inside = tiles.shape[1:]
    tiles = tiles.reshape(*(lax.axis_size(a) for a in axes), *inside)
    tiles = jnp.moveaxis(tiles, turns, range(len(axes))).reshape(-1, *inside)
    for k in turns:
        tiles = lax.psum_scatter(tiles, axes[k], scatter_dimension=0, tiled=True)
    return tiles[0]


def sum_by_axis(x, axes, turns, dim):
    size = lax.axis_size(axes)
    return reduced_to_own(in_blocks(x, dim, size), axes, turns)


def sent_and_summed(x, axis, dim):
    tiles = in_blocks(x, dim, lax.axis_size(axis))
    arrived = lax.all_to_all(tiles, axis, split_axis=0, concat_axis=0, tiled=True)
    return arrived.astype(jnp.float32).sum(axis=0)


def joined_along(tiles, dim):
    lengths = list(tiles.shape[1:])
    lengths[dim] *= tiles.shape[0]
    return jnp.moveaxis(tiles, 0, dim).reshape(lengths)


def sent_to_all(x, axis):
    size = lax.axis_size(axis)
    return lax.all_to_all(jnp.broadcast_to(x[None], (size, *x.shape)), axis, 0, 0, tiled=True)


def gathered_copies(x, axis, dim):
    return joined_along(sent_to_all(x, axis), dim)


def normalize(widened, norm_gain):
    factor = lax.rsqrt(jnp.mean(widened * widened, axis=-1, keepdims=True) + EPSILON)
    return widened * factor * norm_gain


def contract_first(left, right):
    return lax.dot_general(
        left, right, (((0,), (0,)), ((), ())), preferred_element_type=jnp.float32
    )


def contract_last(left, right):
    return lax.dot_general(
        left, right, (((1,), (1,)), ((), ())), preferred_element_type=jnp.float32
    )


def local(tokens, cotangent, norm_gain, gate_weight, up_weight, down_weight, depths):
    parts = lax.axis_size("fsdp")
    place = lax.axis_index("fsdp")
    rows_here = tokens.shape[0]
    own_rows = rows_here // parts
    active = depths > REC
    widened = tokens.astype(jnp.float32)
    normed = normalize(widened, norm_gain).astype(jnp.bfloat16)
    masked = jnp.where(active[:, None], cotangent, jnp.zeros_like(cotangent))
    ordinal = jnp.cumsum(active.astype(jnp.int32)) - 1
    selector = (ordinal[None, :] == jnp.arange(MAXACT, dtype=jnp.int32)[:, None]) & active[None, :]
    picker = selector.astype(jnp.bfloat16)
    send_normed = jnp.dot(picker, normed, preferred_element_type=jnp.float32).astype(jnp.bfloat16)
    send_masked = jnp.dot(picker, masked, preferred_element_type=jnp.float32).astype(jnp.bfloat16)
    source = jnp.dot(selector.astype(jnp.float32), widened, precision=lax.Precision.HIGHEST)
    all_normed, all_masked = side_by_side((send_normed, send_masked), SEQ, 0, 1)
    gate = jnp.dot(all_normed, gate_weight, preferred_element_type=jnp.float32)
    up = jnp.dot(all_normed, up_weight, preferred_element_type=jnp.float32)
    sigmoid_gate = jax.nn.sigmoid(gate)
    swished = gate * sigmoid_gate
    hidden = (swished * up).astype(jnp.bfloat16)
    hidden_grad = contract_last(all_masked, down_weight)
    gate_rows = (hidden_grad * up * sigmoid_gate * (1.0 + gate * (1.0 - sigmoid_gate))).astype(
        jnp.bfloat16
    )
    up_rows = (hidden_grad * swished).astype(jnp.bfloat16)
    gate_term = contract_first(all_normed, gate_rows)
    up_term = contract_first(all_normed, up_rows)
    down_term = contract_first(hidden, all_masked)
    grads = tuple(
        (
            part.astype(jnp.float32)
            for part in sum_together(
                (
                    gate_term.astype(jnp.bfloat16),
                    up_term.astype(jnp.bfloat16),
                    down_term.astype(jnp.bfloat16),
                ),
                "rep",
                (0, 0, 1),
            )
        )
    )
    slot_count = send_normed.shape[0]
    share = slot_count // parts
    seq_summed = sum_by_axis(
        (contract_last(gate_rows, gate_weight) + contract_last(up_rows, up_weight)).astype(
            jnp.bfloat16
        ),
        SEQ,
        (1, 0),
        0,
    ).astype(jnp.float32)
    feature_grad = sent_and_summed(seq_summed.astype(jnp.bfloat16), "fsdp", 0)
    mine = lax.dynamic_slice_in_dim(source, place * share, share, 0)
    _, pullback = jax.vjp(partial(normalize, norm_gain=norm_gain), mine)
    slot_grad = pullback(feature_grad)[0].astype(jnp.bfloat16)
    every_slot = gathered_copies(slot_grad, "fsdp", 0)
    own_columns = lax.dynamic_slice_in_dim(picker, place * own_rows, own_rows, 1)
    branch_grad = contract_first(own_columns, every_slot).astype(jnp.bfloat16)
    return (branch_grad, grads[0], grads[1], grads[2])


def solution(mesh):
    split = Mesh(
        mesh.devices.reshape(mesh.shape["rep"], 12, 2, mesh.shape["fsdp"]),
        ("rep", "seq_0", "seq_1", "fsdp"),
    )
    in_specs = (
        P(REP_SEQ, None),
        P(REP_SEQ, None),
        P(),
        P(None, SEQ_FSDP),
        P(None, SEQ_FSDP),
        P(SEQ_FSDP, None),
        P(REP_SEQ),
    )
    out_specs = (P(REP_SEQ_FSDP, None), P("rep", SEQ_FSDP), P("rep", SEQ_FSDP), P(SEQ_FSDP, "rep"))
    return jax.shard_map(local, mesh=split, in_specs=in_specs, out_specs=out_specs, check_vma=False)
```

profile of v0, /device:TPU:1, one launch (start us, length us, event | category | flops | bytes accessed | tf_op | source)
XLA Modules:
  0.0 229.2 jit_solution(17180451903844074464)
XLA Ops:
  7.2 2.2 fusion.1
  10.8 2.0 convolution_convert_fusion.4
  14.3 69.3 %all-gather.2.cloned.1.call-done = bf16[192,8192]{1,0:T(8,128)(2,1)} async-done(((bf16[8,8192]{1,0:T(8,128)(2,1)}), bf16[192,8192]{1,0:T(8,128)(2,1)}) %all-gather.2.cloned.1.call-update) | async-done | bytes 3145744 | tf_op jit(solution)/shard_map/all_gather | solution.py:26
  83.5 2.1 fusion.15
  85.7 2.3 fusion.17
  89.8 1.2 copy.11
  91.1 2.0 convolution_convert_fusion
  93.1 1.4 copy.12
  94.5 1.8 convolution_convert_fusion.2
  96.3 2.7 %reshape_reshape.10 = bf16[8,65536]{1,0:T(8,128)(2,1)} reshape(bf16[4096,128]{1,0:T(8,128)(2,1)} %convolution_convert_fusion.2) | data formatting | bytes 2097152 | tf_op jit(solution)/shard_map/reshape;reshape | solution.py:38
  99.0 3.2 %convolution_convert_fusion.1 = bf16[4096,128]{1,0:T(8,128)(2,1)} fusion(bf16[192,128]{1,0:T(8,128)(2,1)S(1)} %get-tuple-element.11, bf16[192,8192]{1,0:T(8,128)(2,1)} %all-gather.2.cloned.1.call-done), kind=kOutput, calls=%fused_computation.5 | convolution fusion | flops 201850880 | bytes 2670592 | tf_op jit(solution)/shard_map/dot_general | solution.py:90
  102.2 2.6 %reshape_reshape.11 = bf16[8,65536]{1,0:T(8,128)(2,1)} reshape(bf16[4096,128]{1,0:T(8,128)(2,1)} %convolution_convert_fusion.1) | data formatting | bytes 2097152 | tf_op jit(solution)/shard_map/reshape;reshape | solution.py:38
  104.8 4.9 %reduce-scatter.4.cloned.1.call-done = bf16[12,8,4096]{2,1,0:T(8,128)(2,1)} async-done(((bf16[24,8,4096]{2,1,0:T(8,128)(2,1)}), bf16[12,8,4096]{2,1,0:T(8,128)(2,1)}) %reduce-scatter.4.cloned.1.call-update) | async-done | bytes 786448 | tf_op jit(solution)/shard_map/reduce_scatter | solution.py:54
  109.8 5.3 %pad_maximum_fusion = bf16[8,196608]{1,0:T(8,128)(2,1)} fusion(bf16[8,65536]{1,0:T(8,128)(2,1)} %bitcast.27, bf16[8,65536]{1,0:T(8,128)(2,1)} %reshape_reshape.11, bf16[8,65536]{1,0:T(8,128)(2,1)} %reshape_reshape.10), kind=kLoop, calls=%fused_computation.13 | loop fusion | flops 9437184 | bytes 6291456 | tf_op jit(solution)/shard_map/concatenate | solution.py:38
  115.1 5.0 %reshape.101 = bf16[12288,128]{1,0:T(8,128)(2,1)} reshape(bf16[8,196608]{1,0:T(8,128)(2,1)} %pad_maximum_fusion) | data formatting | bytes 6291456 | tf_op jit(solution)/shard_map/reshape | solution.py:40
  120.1 42.7 %reduce-scatter.6.cloned.1.call-done = bf16[1,8,4096]{2,1,0:T(8,128)(2,1)} async-done(((bf16[12,8,4096]{2,1,0:T(8,128)(2,1)}), bf16[1,8,4096]{2,1,0:T(8,128)(2,1)}) %reduce-scatter.6.cloned.1.call-update) | async-done | bytes 65552 | tf_op jit(solution)/shard_map/reduce_scatter | solution.py:54
  162.8 1.5 reshape.97
  164.3 3.5 %all-to-all-start = ((bf16[4,2,4096]{2,1,0:T(2,128)(2,1)}), bf16[4,2,4096]{2,1,0:T(2,128)(2,1)S(1)}, u32[]{:S(2)}, u32[]{:S(2)}) async-start(bf16[4,2,4096]{2,1,0:T(2,128)(2,1)} %reshape.97), calls=%async_computation.2 | async-start | bytes 131072 | tf_op jit(solution)/shard_map/all_to_all | solution.py:65
  168.2 4.1 %all-to-all-done = bf16[4,2,4096]{2,1,0:T(2,128)(2,1)S(1)} async-done(((bf16[4,2,4096]{2,1,0:T(2,128)(2,1)}), bf16[4,2,4096]{2,1,0:T(2,128)(2,1)S(1)}, u32[]{:S(2)}, u32[]{:S(2)}) %all-to-all-start) | async-done | bytes 65568 | tf_op jit(solution)/shard_map/all_to_all | solution.py:65
  173.3 3.3 %all-to-all-start.1 = ((bf16[4,2,4096]{2,1,0:T(2,128)(2,1)}), bf16[4,2,4096]{2,1,0:T(2,128)(2,1)S(1)}, u32[]{:S(2)}, u32[]{:S(2)}) async-start(bf16[4,2,4096]{2,1,0:T(2,128)(2,1)} %broadcast_in_dim.17), calls=%async_computation.3 | async-start | bytes 131072 | tf_op jit(solution)/shard_map/all_to_all | solution.py:77
  176.6 4.5 %all-to-all-done.1 = bf16[4,2,4096]{2,1,0:T(2,128)(2,1)S(1)} async-done(((bf16[4,2,4096]{2,1,0:T(2,128)(2,1)}), bf16[4,2,4096]{2,1,0:T(2,128)(2,1)S(1)}, u32[]{:S(2)}, u32[]{:S(2)}) %all-to-all-start.1) | async-done | bytes 65568 | tf_op jit(solution)/shard_map/all_to_all | solution.py:77
  181.2 1.2 convolution_convert_fusion.3
  182.4 37.7 %reduce-scatter.8.cloned.1.call-done = bf16[1536,128]{1,0:T(8,128)(2,1)} async-done(((bf16[12288,128]{1,0:T(8,128)(2,1)}), bf16[1536,128]{1,0:T(8,128)(2,1)}) %reduce-scatter.8.cloned.1.call-update) | async-done | bytes 393232 | tf_op jit(solution)/shard_map/reduce_scatter | solution.py:41
  220.1 1.9 slice_convert_fusion
  (43 shorter events, 6.9 us)
Async XLA Ops:
  7.2 76.4 %copy-start = (bf16[4096,128]{1,0:T(8,128)(2,1)S(1)}, bf16[4096,128]{1,0:T(8,128)(2,1)}, u32[]{:S(2)}) copy-start(bf16[4096,128]{1,0:T(8,128)(2,1)} %param.10) | copy-start | bytes 3145732
  7.2 5.7 %copy-start.1 = (bf16[256,4096]{1,0:T(8,128)(2,1)S(1)}, bf16[256,4096]{1,0:T(8,128)(2,1)}, u32[]{:S(2)}) copy-start(bf16[256,4096]{1,0:T(8,128)(2,1)} %param.7) | copy-start | bytes 6291460
  7.2 5.6 %copy-start.5 = (f32[4096]{0:T(1024)S(1)}, f32[4096]{0:T(1024)}, u32[]{:S(2)}) copy-start(f32[4096]{0:T(1024)} %param.9) | copy-start | bytes 49156
  7.2 76.3 %all-gather.2.cloned.1.call-start = ((), (), s32[]{:S(2)}) async-start(), calls=%async_computation.5 | async-start | bytes 3276800 | tf_op jit(solution)/shard_map/all_gather | solution.py:26
  14.2 95.6 %reduce-scatter.4.cloned.1.call-start = ((), (), s32[]{:S(2)}) async-start(), calls=%async_computation.6 | async-start | bytes 2359296 | tf_op jit(solution)/shard_map/reduce_scatter | solution.py:54
  83.5 4.4 %copy-start.2 = (bf16[192,8192]{1,0:T(8,128)(2,1)S(1)}, bf16[192,8192]{1,0:T(8,128)(2,1)}, u32[]{:S(2)}) copy-start(bf16[192,8192]{1,0:T(8,128)(2,1)} %all-gather.2.cloned.1.call-done) | copy-start | bytes 9437188
  83.5 4.4 %copy-start.6 = (bf16[128,4096]{1,0:T(8,128)(2,1)S(1)}, bf16[128,4096]{1,0:T(8,128)(2,1)}, u32[]{:S(2)}) copy-start(bf16[128,4096]{1,0:T(8,128)(2,1)} %param.12) | copy-start | bytes 3145732
  87.9 1.2 copy-start.4
  91.0 71.8 %reduce-scatter.6.cloned.1.call-start = ((), (), s32[]{:S(2)}) async-start(), calls=%async_computation.7 | async-start | bytes 851968 | tf_op jit(solution)/shard_map/reduce_scatter | solution.py:54
  91.1 3.5 %copy-start.3 = (bf16[192,8192]{1,0:T(8,128)(2,1)S(1)}, bf16[192,8192]{1,0:T(8,128)(2,1)}, u32[]{:S(2)}) copy-start(bf16[192,8192]{1,0:T(8,128)(2,1)} %all-gather.2.cloned.1.call-done) | copy-start | bytes 9437188
  109.8 110.3 %reduce-scatter.8.cloned.1.call-start = ((), (), s32[]{:S(2)}) async-start(), calls=%async_computation.8 | async-start | bytes 3538944 | tf_op jit(solution)/shard_map/reduce_scatter | solution.py:41
  164.3 7.9 %all-to-all-start = ((bf16[4,2,4096]{2,1,0:T(2,128)(2,1)}), bf16[4,2,4096]{2,1,0:T(2,128)(2,1)S(1)}, u32[]{:S(2)}, u32[]{:S(2)}) async-start(bf16[4,2,4096]{2,1,0:T(2,128)(2,1)} %reshape.97), calls=%async_computation.2 | async-start | bytes 131072 | tf_op jit(solution)/shard_map/all_to_all | solution.py:65
  173.3 7.8 %all-to-all-start.1 = ((bf16[4,2,4096]{2,1,0:T(2,128)(2,1)}), bf16[4,2,4096]{2,1,0:T(2,128)(2,1)S(1)}, u32[]{:S(2)}, u32[]{:S(2)}) async-start(bf16[4,2,4096]{2,1,0:T(2,128)(2,1)} %broadcast_in_dim.17), calls=%async_computation.3 | async-start | bytes 131072 | tf_op jit(solution)/shard_map/all_to_all | solution.py:77
Sparse Core Ops, SparseCore 0:
  14.3 69.1 all-gather.1
  91.1 18.5 reduce-scatter.3
  113.2 49.5 reduce-scatter.5
  165.8 54.2 reduce-scatter.7
where the time goes:
time: 232 us; the launch traced here: 229 us
  waiting for transfers between devices  163 us (70%)
  matrix products  17.4 us (7%)
  local copies, waits for them, and re-layouts  16.2 us (7%)
  between operations  13.9 us (6%)
  other arithmetic  11.5 us (5%)
  starting transfers between devices  6.91 us (3%)
    all_gather x1, waiting for transfers between devices, side_by_side(): lax.all_gather(both, axis, axis=dim, tiled=True)  69.3 us
    reduce_scatter x2, waiting for transfers between devices, reduced_to_own(): tiles = lax.psum_scatter(tiles, axes[k], scatter_dimension=0, tiled=True)  47.6 us
    reduce_scatter x1, waiting for transfers between devices, sum_together(): lax.psum_scatter(lines, axis, tiled=True).reshape(-1)  37.7 us
    dot_general x4, matrix products, contract_first(): lax.dot_general(left, right, (((0,), (0,)), ((), ())), preferred_element_...  8.25 us
    another operation x2, local copies, waits for them, and re-layouts, sum_together(): lines = jnp.concatenate([b.reshape(size, -1) for b in tiles], axis=1)  5.3 us
    concatenate x1, other arithmetic, sum_together(): lines = jnp.concatenate([b.reshape(size, -1) for b in tiles], axis=1)  5.26 us
    reshape x1, local copies, waits for them, and re-layouts, sum_together(): jnp.pad(lines, ((0, 0), (0, width * 128 - lines.shape[1]))).reshape(-1, 128)  4.96 us
  transfers between devices with their start and end apart: 6, of which 6 were waited for; matrix products, arithmetic and copies ran while one was open for 12% of the time, Pallas kernels for 0%

commit v1 on v0

v1 whole, which is shorter than its diff:
```python
import functools

import jax
import jax.numpy as jnp
from jax import lax
from jax.experimental import pallas as pl
from jax.experimental.pallas import tpu as pltpu
from jax.sharding import PartitionSpec as P

REC = 1
SLOTS = 8
EPSILON = 1e-05
MESH = pl.DeviceIdType.MESH
BF = jnp.bfloat16
F32 = jnp.float32


def dot(a, b, da=1, db=0):
    return lax.dot_general(a, b, (((da,), (db,)), ((), ())), preferred_element_type=F32)


def remote(src, dst, ssem, rsem, device):
    return pltpu.make_async_remote_copy(
        src_ref=src,
        dst_ref=dst,
        send_sem=ssem,
        recv_sem=rsem,
        device_id=device,
        device_id_type=MESH,
    )


class PlaneGather:
    def __init__(self, buf, sems, where, sizes, device, sent):
        self.buf, self.sent, self.device = buf, sent, device
        self.zs, self.zr, self.xs, self.xr, self.cs, self.cr = sems
        self.y, self.z, self.c, self.x = where
        self.Y, self.Z, self.X = sizes
        self.p = lax.rem(self.x, 2)
        self.right, self.left = self.Z // 2, (self.Z - 1) // 2
        self.here = device(self.y, self.z, self.c, self.x)

    def zz(self, way, s):
        return lax.rem(self.z + (self.Z - s if way == 0 else s), self.Z)

    def go(self, copy):
        copy.start()
        self.sent.append(copy)

    def forward(self, way, s, block):
        step = 1 if way == 0 else self.Z - 1
        to = self.device(self.y, lax.rem(self.z + step, self.Z), self.c, self.x)
        part = self.buf.at[block, self.c, self.p]
        self.go(remote(part, part, self.zs.at[way, s], self.zr.at[way, s], to))

    def to_core(self, part, way, s, kind):
        to = self.device(self.y, self.z, 1 - self.c, self.x)
        self.go(remote(part, part, self.cs.at[way, s, kind], self.cr.at[way, s, kind], to))

    def start(self):
        self.forward(0, 1, self.z)
        if self.left:
            self.forward(1, 1, self.z)
        self.to_core(self.buf.at[self.z, self.c], 0, 0, 0)

    def arrive_one(self, way, s, last):
        block = self.zz(way, s)
        part = self.buf.at[block, self.c, self.p]
        remote(part, part, self.zs.at[way, s], self.zr.at[way, s], self.here).wait_recv()
        if s < last:
            self.forward(way, s + 1, block)
        for q in range(2):
            xx = lax.rem(self.x + (1 if q == 0 else self.X - 1), self.X)
            to = self.device(self.y, self.z, self.c, xx)
            quarter = self.buf.at[block, self.c, self.p, q]
            self.go(remote(quarter, quarter, self.xs.at[way, s, q], self.xr.at[way, s, q], to))
        self.to_core(part, way, s, 0)

    def beside_one(self, way, s):
        block = self.zz(way, s)
        for q in range(2):
            quarter = self.buf.at[block, self.c, 1 - self.p, q]
            remote(
                quarter, quarter, self.xs.at[way, s, q], self.xr.at[way, s, q], self.here
            ).wait_recv()
        self.to_core(self.buf.at[block, self.c, 1 - self.p], way, s, 1)

    def arrive(self, s):
        if 1 <= s <= self.right:
            self.arrive_one(0, s, self.right)
        if 1 <= s <= self.left:
            self.arrive_one(1, s, self.left)
        if 1 <= s - 1 <= self.right:
            self.beside_one(0, s - 1)
        if 1 <= s - 1 <= self.left:
            self.beside_one(1, s - 1)

    def finish(self):
        part = self.buf.at[self.z, 1 - self.c]
        remote(part, part, self.cs.at[0, 0, 0], self.cr.at[0, 0, 0], self.here).wait_recv()
        for way, last in ((0, self.right), (1, self.left)):
            for s in range(1, last + 1):
                block = self.zz(way, s)
                for kind in range(2):
                    h = self.p if kind == 0 else 1 - self.p
                    part = self.buf.at[block, 1 - self.c, h]
                    remote(
                        part, part, self.cs.at[way, s, kind], self.cr.at[way, s, kind], self.here
                    ).wait_recv()


def kernel(
    sizes,
    tok_hbm,
    cot_hbm,
    gain_ref,
    gw_hbm,
    uw_hbm,
    dw_hbm,
    dep_ref,
    out_b,
    out_g,
    out_u,
    out_d,
    tok,
    cot,
    wgu,
    dw,
    source,
    picks,
    G,
    H,
    S,
    R,
    FAs,
    FAr,
    FO,
    FBs,
    FBr,
    FT,
    FCs,
    FCr,
    FDr,
    lsem,
    gsems,
    hsems,
    asems,
    ysems,
    fsems,
):
    Y, Z, X = sizes
    n_tok, D = tok.shape
    ff = dw.shape[0]
    N = Z * 2 * SLOTS
    QD, HD, CW = D // 4, D // (4 * Y), D // (2 * X)
    y, x = lax.axis_index("rep"), lax.axis_index("fsdp")
    seq = lax.axis_index("seq")
    z, c = seq // 2, lax.rem(seq, 2)

    def device(yy, zz, cc, xx):
        return (yy, zz * 2 + cc, xx)

    loads = [
        pltpu.make_async_copy(tok_hbm, tok, lsem.at[0]),
        pltpu.make_async_copy(cot_hbm, cot, lsem.at[1]),
        pltpu.make_async_copy(gw_hbm, wgu.at[:, 0:ff], lsem.at[2]),
        pltpu.make_async_copy(uw_hbm, wgu.at[:, ff : 2 * ff], lsem.at[3]),
        pltpu.make_async_copy(dw_hbm, dw, lsem.at[4]),
    ]
    for load in loads:
        load.start()

    partners = [device(lax.rem(y + d, Y), z, c, x) for d in range(1, Y)]
    partners += [device(y, lax.rem(z + d, Z), c, x) for d in range(1, Z)]
    mine = c * X + x

    def corner(d):
        j = lax.rem(mine + d, 2 * X)
        return device(y, z, j // X, lax.rem(j, X))

    partners += [corner(d) for d in range(1, 2 * X)]
    barrier = pltpu.get_barrier_semaphore()
    for partner in partners:
        pl.semaphore_signal(barrier, inc=1, device_id=partner, device_id_type=MESH)

    act = jnp.where(dep_ref[...] > REC, 1.0, 0.0).astype(F32)
    act = jnp.broadcast_to(act, (16, n_tok))
    before = lax.broadcasted_iota(jnp.int32, (n_tok, n_tok), 0)
    after = lax.broadcasted_iota(jnp.int32, (n_tok, n_tok), 1)
    tri = jnp.where(before <= after, 1.0, 0.0).astype(BF)
    ordinal = dot(act.astype(BF), tri) - 1.0
    slot = lax.broadcasted_iota(jnp.int32, (16, n_tok), 0).astype(F32)
    sel = jnp.where((ordinal == slot) & (act > 0.5), 1.0, 0.0).astype(BF)
    own = n_tok // X
    i0 = lax.broadcasted_iota(jnp.int32, (own, n_tok), 0)
    i1 = lax.broadcasted_iota(jnp.int32, (own, n_tok), 1)
    rows = jnp.where(i1 == i0 + x * own, 1.0, 0.0).astype(BF)
    picks[...] = dot(rows, sel, 1, 1).astype(BF)
    loads[0].wait()
    tsel = dot(sel, tok[...])
    factor = lax.rsqrt(jnp.mean(tsel * tsel, axis=-1, keepdims=True) + EPSILON)
    normed = tsel * factor * gain_ref[...]
    source[...] = tsel[:SLOTS]
    loads[1].wait()
    csel = dot(sel, cot[...])
    block = jnp.concatenate([normed[:SLOTS], csel[:SLOTS]], axis=0).astype(BF)
    for h in range(2):
        for q in range(2):
            at = (h * 2 + q) * QD
            G[z, c, h, q] = block[:, at : at + QD]
    for yy in range(Y):
        for h in range(2):
            for q in range(2):
                at = (yy * 4 + h * 2 + q) * HD
                S[yy, h, q] = block[:, at : at + HD]
    for h in range(2):
        for q in range(2):
            H[z, c, h, q, y] = S[y, h, q]

    pl.semaphore_wait(barrier, len(partners))

    sent = []

    def go(copy):
        copy.start()
        sent.append(copy)

    where = (y, z, c, x)
    gather = PlaneGather(G, gsems, where, sizes, device, sent)
    gather.start()
    as_, ar = asems
    for d in range(1, Y):
        yy = lax.rem(y + d, Y)
        go(
            remote(
                S.at[yy], H.at[z, c, :, :, y], as_.at[d], ar.at[d], device(yy, z, c, x)
            )
        )
    for s in range(1, gather.right + 1):
        gather.arrive(s)
    gather.arrive(gather.right + 1)
    for d in range(1, Y):
        yy = lax.rem(y + Y - d, Y)
        part = H.at[z, c, :, :, yy]
        remote(S.at[yy], part, as_.at[d], ar.at[d], device(y, z, c, x)).wait_recv()
    wide = PlaneGather(H, hsems, where, sizes, device, sent)
    wide.start()
    gather.finish()

    for load in loads[2:]:
        load.wait()
    gu = jnp.zeros((2 * N, 2 * ff), F32)
    hd = jnp.zeros((2 * N, ff), F32)
    for h in range(2):
        for q in range(2):
            at = (h * 2 + q) * QD
            a = G[:, :, h, q].reshape(2 * N, QD)
            gu += dot(a, wgu[at : at + QD, :])
            hd += dot(a, dw[:, at : at + QD], 1, 1)
    gu = gu.reshape(Z * 2, 2, SLOTS, 2 * ff)[:, 0].reshape(N, 2 * ff)
    hg = hd.reshape(Z * 2, 2, SLOTS, ff)[:, 1].reshape(N, ff)
    gate, up = gu[:, :ff], gu[:, ff:]
    sig = jax.nn.sigmoid(gate)
    swished = gate * sig
    hidden = (swished * up).astype(BF)
    gate_rows = (hg * up * sig * (1.0 + gate * (1.0 - sig))).astype(BF)
    up_rows = (hg * swished).astype(BF)
    for k in range(2):
        half = slice(k * N // 2, (k + 1) * N // 2)
        R[y, k, 0] = gate_rows[half]
        R[y, k, 1] = up_rows[half]
        R[y, k, 2] = hidden[half]

    ys, yr = ysems

    def y_forward(way, k, unit):
        step = 1 if way == 0 else Y - 1
        to = device(lax.rem(y + step, Y), z, c, x)
        part = R.at[unit] if k < Y // 2 else R.at[unit, way]
        go(remote(part, part, ys.at[way, k], yr.at[way, k], to))

    def y_arrive(k):
        for way in range(2):
            unit = lax.rem(y + (Y - k if way == 0 else k), Y)
            part = R.at[unit] if k < Y // 2 else R.at[unit, way]
            remote(part, part, ys.at[way, k], yr.at[way, k], device(y, z, c, x)).wait_recv()
            if k < Y // 2:
                y_forward(way, k + 1, unit)

    for way in range(2):
        y_forward(way, 1, y)

    wide.arrive(1)

    f_as, f_ar, f_bs, f_br, f_cs, f_cr, f_ds, f_dr = fsems
    both = jnp.concatenate([gate_rows, up_rows], axis=1)
    other = device(y, z, 1 - c, x)
    for d in range(X):
        at = pl.multiple_of(((1 - c) * X + d) * CW, CW)
        FAs[d] = dot(both, wgu[pl.ds(at, CW), :], 1, 1).astype(BF)
        go(remote(FAs.at[d], FAr.at[d], f_as.at[d], f_ar.at[d], other))
    wide.arrive(2)
    for d in range(X):
        at = pl.multiple_of((c * X + d) * CW, CW)
        FO[d] = dot(both, wgu[pl.ds(at, CW), :], 1, 1)
    wide.arrive(3)
    for d in range(X):
        remote(FAs.at[d], FAr.at[d], f_as.at[d], f_ar.at[d], other).wait_recv()
    for d in range(1, X):
        xx = lax.rem(x + d, X)
        FBs[d] = (FO[xx] + FAr[xx].astype(F32)).astype(BF)
        go(remote(FBs.at[d], FBr.at[d], f_bs.at[d], f_br.at[d], device(y, z, c, xx)))
    for s in range(4, gather.right + 2):
        wide.arrive(s)
    total = FO[x] + FAr[x].astype(F32)
    for d in range(1, X):
        remote(FBs.at[d], FBr.at[d], f_bs.at[d], f_br.at[d], other).wait_recv()
        total += FBr[d].astype(F32)
    FT[...] = total.reshape(Z, 16, CW)
    FCs[...] = total.astype(BF).reshape(Z, 16, CW)
    for d in range(1, Z):
        zz = lax.rem(z + d, Z)
        go(remote(FCs.at[zz], FCr.at[d], f_cs.at[d], f_cr.at[d], device(y, zz, c, x)))
    if Y > 2:
        y_arrive(1)
    total = FT[z]
    for d in range(1, Z):
        remote(FCs.at[z], FCr.at[d], f_cs.at[d], f_cr.at[d], other).wait_recv()
        total += FCr[d].astype(F32)
    FDr[mine] = total.astype(BF)
    for d in range(1, 2 * X):
        go(remote(FDr.at[mine], FDr.at[mine], f_ds.at[d], f_dr.at[d], corner(d)))
    wide.finish()

    def accumulate(unit, first):
        rows_g = jnp.concatenate([R[unit, 0, 0], R[unit, 1, 0]], axis=0)
        rows_u = jnp.concatenate([R[unit, 0, 1], R[unit, 1, 1]], axis=0)
        rows_h = jnp.concatenate([R[unit, 0, 2], R[unit, 1, 2]], axis=0)
        gu_rows = jnp.concatenate([rows_g, rows_u], axis=1)
        for h in range(2):
            for q in range(2):
                at = (h * 2 + q) * HD
                a = H[:, :, h, q, unit].astype(F32).reshape(Z * 2, 2, SLOTS, HD)
                nrm = a[:, 0].reshape(N, HD).astype(BF)
                msk = a[:, 1].reshape(N, HD).astype(BF)
                pair = dot(nrm, gu_rows, 0, 0)
                down = dot(rows_h, msk, 0, 0)
                if first:
                    out_g[at : at + HD, :] = pair[:, :ff]
                    out_u[at : at + HD, :] = pair[:, ff:]
                    out_d[:, at : at + HD] = down
                else:
                    out_g[at : at + HD, :] += pair[:, :ff]
                    out_u[at : at + HD, :] += pair[:, ff:]
                    out_d[:, at : at + HD] += down

    def accumulate_pair(k):
        accumulate(lax.rem(y + Y - k, Y), False)
        if k < Y // 2:
            accumulate(lax.rem(y + k, Y), False)

    accumulate(y, True)
    done = 1
    for k in range(2, Y // 2):
        y_arrive(k)
        accumulate_pair(done)
        done = k

    for d in range(1, 2 * X):
        j = lax.rem(mine + 2 * X - d, 2 * X)
        remote(FDr.at[j], FDr.at[j], f_ds.at[d], f_dr.at[d], other).wait_recv()
    pieces = []
    for j in range(2 * X):
        piece = FDr[j].astype(F32)
        pieces.append(jnp.where(c == 0, piece[:SLOTS], piece[SLOTS:]))
    feature = jnp.concatenate(pieces, axis=1)
    src = source[...]
    scale = lax.rsqrt(jnp.mean(src * src, axis=-1, keepdims=True) + EPSILON)
    weighted = feature * gain_ref[...]
    along = jnp.mean(weighted * src, axis=-1, keepdims=True)
    grad = weighted * scale - src * (scale * scale * scale * along)
    grad = jnp.concatenate([grad, jnp.zeros_like(grad)], axis=0).astype(BF)
    out_b[...] = dot(picks[...], grad).astype(BF)

    while done < Y // 2 - 1:
        done += 1
        accumulate_pair(done - 1)
    if Y > 2:
        accumulate_pair(done)
    y_arrive(Y // 2)
    accumulate_pair(Y // 2)
    for copy in sent:
        copy.wait_send()


def local(sizes, tokens, cotangent, norm_gain, gate_weight, up_weight, down_weight, depths):
    Y, Z, X = sizes
    n_tok, D = tokens.shape
    ff = gate_weight.shape[1]
    N = Z * 2 * SLOTS
    QD, HD, CW = D // 4, D // (4 * Y), D // (2 * X)
    vmem, dma = pltpu.VMEM, pltpu.SemaphoreType.DMA
    steps = Z // 2 + 1
    plane = (
        dma((2, steps)),
        dma((2, steps)),
        dma((2, steps, 2)),
        dma((2, steps, 2)),
        dma((2, steps, 2)),
        dma((2, steps, 2)),
    )
    hbm, whole = pl.BlockSpec(memory_space=pl.ANY), pl.BlockSpec(memory_space=pltpu.VMEM)
    return pl.pallas_call(
        functools.partial(kernel, sizes),
        out_shape=(
            jax.ShapeDtypeStruct((n_tok // X, D), BF),
            jax.ShapeDtypeStruct((D // Y, ff), F32),
            jax.ShapeDtypeStruct((D // Y, ff), F32),
            jax.ShapeDtypeStruct((ff, D // Y), F32),
        ),
        in_specs=[hbm, hbm, whole, hbm, hbm, hbm, whole],
        out_specs=(whole,) * 4,
        scratch_shapes=[
            vmem((n_tok, D), BF),
            vmem((n_tok, D), BF),
            vmem((D, 2 * ff), BF),
            vmem((ff, D), BF),
            vmem((SLOTS, D), F32),
            vmem((n_tok // X, 16), BF),
            vmem((Z, 2, 2, 2, 16, QD), BF),
            vmem((Z, 2, 2, 2, Y, 16, HD), BF),
            vmem((Y, 2, 2, 16, HD), BF),
            vmem((Y, 2, 3, N // 2, ff), BF),
            vmem((X, N, CW), BF),
            vmem((X, N, CW), BF),
            vmem((X, N, CW), F32),
            vmem((X, N, CW), BF),
            vmem((X, N, CW), BF),
            vmem((Z, 16, CW), F32),
            vmem((Z, 16, CW), BF),
            vmem((Z, 16, CW), BF),
            vmem((2 * X, 16, CW), BF),
            dma((5,)),
            plane,
            plane,
            (dma((Y,)), dma((Y,))),
            (dma((2, Y // 2 + 1)), dma((2, Y // 2 + 1))),
            (
                dma((X,)),
                dma((X,)),
                dma((X,)),
                dma((X,)),
                dma((Z,)),
                dma((Z,)),
                dma((2 * X,)),
                dma((2 * X,)),
            ),
        ],
        compiler_params=pltpu.CompilerParams(
            collective_id=0, has_side_effects=True, vmem_limit_bytes=58 * 1024 * 1024
        ),
    )(
        tokens,
        cotangent,
        norm_gain.reshape(1, D),
        gate_weight,
        up_weight,
        down_weight,
        depths.reshape(1, n_tok),
    )


def solution(mesh):
    sizes = (mesh.shape["rep"], mesh.shape["seq"] // 2, mesh.shape["fsdp"])
    rows, hidden = ("rep", "seq"), ("seq", "fsdp")
    return jax.shard_map(
        functools.partial(local, sizes),
        mesh=mesh,
        in_specs=(
            P(rows, None),
            P(rows, None),
            P(),
            P(None, hidden),
            P(None, hidden),
            P(hidden, None),
            P(rows),
        ),
        out_specs=(
            P(("rep", "seq", "fsdp"), None),
            P("rep", hidden),
            P("rep", hidden),
            P(hidden, "rep"),
        ),
        check_vma=False,
    )
```

time: 232 us -> 100 us (0.43)
  the two profiles are of different devices: /device:TPU:1 before, /device:TPU:24 now
where the time goes in v1:
time: 100 us
  Pallas kernels  93.4 us (93%)
  local copies, waits for them, and re-layouts  5.95 us (6%)
    pallas_call x1, Pallas kernels, local(): pl.pallas_call(functools.partial(kernel, sizes), out_shape=(jax.ShapeDtyp...  93.4 us
    unnamed x6, local copies, waits for them, and re-layouts  5.95 us

profile of v1, /device:TPU:24, one launch (start us, length us, event | category | flops | bytes accessed | tf_op | source)
XLA Modules:
  0.0 100.0 jit_solution(13364758627472638694)
XLA Ops:
  0.6 93.4 %shard_map.102 = (bf16[64,4096]{1,0:T(8,128)(2,1)}, f32[512,128]{1,0:T(8,128)}, f32[512,128]{1,0:T(8,128)}, f32[128,512]{1,0:T(8,128)}) custom-call(bf16[256,4096]{1,0:T(8,128)(2,1)} %tok_hbm.1, bf16[256,4096]{1,0:T(8,128)(2,1)} %cot_hbm.1, f32[1,4096]{1,0:T(1,128)} %bitcast.2, bf16[4096,128]{1,0:T(8,128)(2,1)} %gw_hbm.1, bf16[4096,128]{1,0:T(8,128)(2,1)} %uw_hbm.1, ...), custom_call_target="tpu_custom_call" | custom-call | tf_op jit(solution)/shard_map/pallas_call | solution.py:413
  94.0 0.0 copy-start
  94.0 1.9 %copy.15 = bf16[64,4096]{1,0:T(8,128)(2,1)} copy(bf16[64,4096]{1,0:T(8,128)(2,1)} %get-tuple-element.8) | data formatting | bytes 1048576
  95.9 1.7 %copy.16 = f32[512,128]{1,0:T(8,128)} copy(f32[512,128]{1,0:T(8,128)} %get-tuple-element.9) | data formatting | bytes 524288
  97.6 1.7 %copy.17 = f32[512,128]{1,0:T(8,128)} copy(f32[512,128]{1,0:T(8,128)} %get-tuple-element.10) | data formatting | bytes 524288
  99.3 0.0 copy-done
  99.3 0.7 copy.18
Async XLA Ops:
  94.0 5.3 %copy-start = (f32[128,512]{1,0:T(8,128)S(1)}, f32[128,512]{1,0:T(8,128)}, u32[]{:S(2)}) copy-start(f32[128,512]{1,0:T(8,128)} %get-tuple-element.11) | copy-start | bytes 786436

commit v2 on v1

--- a/solution.py
+++ b/solution.py
@@ -30,6 +30,14 @@
     )
 
 
+def tree(half):
+    return [[s for s in (g + 2, g + 1) if s <= half] for g in range(0, half, 2)]
+
+
+def farthest_first(n):
+    return sorted(range(n), key=lambda d: -min(d, n - d))
+
+
 class PlaneGather:
     def __init__(self, buf, sems, where, sizes, device, sent):
         self.buf, self.sent, self.device = buf, sent, device
@@ -37,8 +45,18 @@
         self.y, self.z, self.c, self.x = where
         self.Y, self.Z, self.X = sizes
         self.p = lax.rem(self.x, 2)
-        self.right, self.left = self.Z // 2, (self.Z - 1) // 2
+        self.half = self.Z // 2
         self.here = device(self.y, self.z, self.c, self.x)
+        self.groups = tree(self.half)
+
+    def events(self):
+        found = []
+        for k, group in enumerate(self.groups):
+            found.append(functools.partial(self.arrive, group[0]))
+            if k:
+                found += [functools.partial(self.beside, s) for s in self.groups[k - 1]]
+            found += [functools.partial(self.arrive, s) for s in group[1:]]
+        return found + [functools.partial(self.beside, s) for s in self.groups[-1]]
 
     def zz(self, way, s):
         return lax.rem(self.z + (self.Z - s if way == 0 else s), self.Z)
@@ -47,63 +65,68 @@
         copy.start()
         self.sent.append(copy)
 
-    def forward(self, way, s, block):
-        step = 1 if way == 0 else self.Z - 1
-        to = self.device(self.y, lax.rem(self.z + step, self.Z), self.c, self.x)
-        part = self.buf.at[block, self.c, self.p]
-        self.go(remote(part, part, self.zs.at[way, s], self.zr.at[way, s], to))
+    def quarters(self, way, s):
+        return (0, 1) if s < self.half else (way,)
+
+    def part(self, way, s, block, c, h):
+        whole = self.buf.at[block, c, h]
+        return whole if s < self.half else self.buf.at[block, c, h, way]
+
+    def forward(self, held, block):
+        for s in (held + 2, held + 1):
+            if s <= self.half:
+                for way in range(2):
+                    step = s - held if way == 0 else self.Z - (s - held)
+                    to = self.device(self.y, lax.rem(self.z + step, self.Z), self.c, self.x)
+                    part = self.part(way, s, block[way], self.c, self.p)
+                    self.go(remote(part, part, self.zs.at[way, s], self.zr.at[way, s], to))
 
     def to_core(self, part, way, s, kind):
         to = self.device(self.y, self.z, 1 - self.c, self.x)
         self.go(remote(part, part, self.cs.at[way, s, kind], self.cr.at[way, s, kind], to))
 
     def start(self):
-        self.forward(0, 1, self.z)
-        if self.left:
-            self.forward(1, 1, self.z)
+        self.forward(0, (self.z, self.z))
         self.to_core(self.buf.at[self.z, self.c], 0, 0, 0)
 
-    def arrive_one(self, way, s, last):
-        block = self.zz(way, s)
-        part = self.buf.at[block, self.c, self.p]
-        remote(part, part, self.zs.at[way, s], self.zr.at[way, s], self.here).wait_recv()
-        if s < last:
-            self.forward(way, s + 1, block)
-        for q in range(2):
-            xx = lax.rem(self.x + (1 if q == 0 else self.X - 1), self.X)
-            to = self.device(self.y, self.z, self.c, xx)
-            quarter = self.buf.at[block, self.c, self.p, q]
-            self.go(remote(quarter, quarter, self.xs.at[way, s, q], self.xr.at[way, s, q], to))
-        self.to_core(part, way, s, 0)
-
-    def beside_one(self, way, s):
-        block = self.zz(way, s)
-        for q in range(2):
-            quarter = self.buf.at[block, self.c, 1 - self.p, q]
+    def arrive(self, s):
+        blocks = (self.zz(0, s), self.zz(1, s))
+        parts = [self.part(way, s, blocks[way], self.c, self.p) for way in range(2)]
+        for way in range(2):
             remote(
-                quarter, quarter, self.xs.at[way, s, q], self.xr.at[way, s, q], self.here
+                parts[way], parts[way], self.zs.at[way, s], self.zr.at[way, s], self.here
             ).wait_recv()
-        self.to_core(self.buf.at[block, self.c, 1 - self.p], way, s, 1)
-
-    def arrive(self, s):
-        if 1 <= s <= self.right:
-            self.arrive_one(0, s, self.right)
-        if 1 <= s <= self.left:
-            self.arrive_one(1, s, self.left)
-        if 1 <= s - 1 <= self.right:
-            self.beside_one(0, s - 1)
-        if 1 <= s - 1 <= self.left:
-            self.beside_one(1, s - 1)
+        if s % 2 == 0:
+            self.forward(s, blocks)
+        for way in range(2):
+            for q in self.quarters(way, s):
+                xx = lax.rem(self.x + (1 if q == 0 else self.X - 1), self.X)
+                to = self.device(self.y, self.z, self.c, xx)
+                quarter = self.buf.at[blocks[way], self.c, self.p, q]
+                self.go(
+                    remote(quarter, quarter, self.xs.at[way, s, q], self.xr.at[way, s, q], to)
+                )
+            self.to_core(parts[way], way, s, 0)
+
+    def beside(self, s):
+        for way in range(2):
+            block = self.zz(way, s)
+            for q in self.quarters(way, s):
+                quarter = self.buf.at[block, self.c, 1 - self.p, q]
+                remote(
+                    quarter, quarter, self.xs.at[way, s, q], self.xr.at[way, s, q], self.here
+                ).wait_recv()
+            self.to_core(self.part(way, s, block, self.c, 1 - self.p), way, s, 1)
 
     def finish(self):
         part = self.buf.at[self.z, 1 - self.c]
         remote(part, part, self.cs.at[0, 0, 0], self.cr.at[0, 0, 0], self.here).wait_recv()
-        for way, last in ((0, self.right), (1, self.left)):
-            for s in range(1, last + 1):
+        for s in range(1, self.half + 1):
+            for way in range(2):
                 block = self.zz(way, s)
                 for kind in range(2):
                     h = self.p if kind == 0 else 1 - self.p
-                    part = self.buf.at[block, 1 - self.c, h]
+                    part = self.part(way, s, block, 1 - self.c, h)
                     remote(
                         part, part, self.cs.at[way, s, kind], self.cr.at[way, s, kind], self.here
                     ).wait_recv()
@@ -118,7 +141,8 @@
     uw_hbm,
     dw_hbm,
     dep_ref,
-    out_b,
+    out_s,
+    out_p,
     out_g,
     out_u,
     out_d,
@@ -127,14 +151,13 @@
     wgu,
     dw,
     source,
-    picks,
     G,
     H,
     S,
     R,
     FAs,
     FAr,
-    FO,
+    B,
     FBs,
     FBr,
     FT,
@@ -195,7 +218,7 @@
     i0 = lax.broadcasted_iota(jnp.int32, (own, n_tok), 0)
     i1 = lax.broadcasted_iota(jnp.int32, (own, n_tok), 1)
     rows = jnp.where(i1 == i0 + x * own, 1.0, 0.0).astype(BF)
-    picks[...] = dot(rows, sel, 1, 1).astype(BF)
+    out_p[...] = dot(rows, sel, 1, 1).astype(BF)
     loads[0].wait()
     tsel = dot(sel, tok[...])
     factor = lax.rsqrt(jnp.mean(tsel * tsel, axis=-1, keepdims=True) + EPSILON)
@@ -236,9 +259,8 @@
                 S.at[yy], H.at[z, c, :, :, y], as_.at[d], ar.at[d], device(yy, z, c, x)
             )
         )
-    for s in range(1, gather.right + 1):
-        gather.arrive(s)
-    gather.arrive(gather.right + 1)
+    for event in gather.events():
+        event()
     for d in range(1, Y):
         yy = lax.rem(y + Y - d, Y)
         part = H.at[z, c, :, :, yy]
@@ -272,60 +294,90 @@
         R[y, k, 2] = hidden[half]
 
     ys, yr = ysems
-
-    def y_forward(way, k, unit):
-        step = 1 if way == 0 else Y - 1
-        to = device(lax.rem(y + step, Y), z, c, x)
-        part = R.at[unit] if k < Y // 2 else R.at[unit, way]
-        go(remote(part, part, ys.at[way, k], yr.at[way, k], to))
+    y_half = Y // 2
+
+    def y_forward(held, units):
+        for k in (held + 2, held + 1):
+            if k <= y_half:
+                for way in range(2):
+                    step = k - held if way == 0 else Y - (k - held)
+                    to = device(lax.rem(y + step, Y), z, c, x)
+                    part = R.at[units[way]] if k < y_half else R.at[units[way], way]
+                    go(remote(part, part, ys.at[way, k], yr.at[way, k], to))
 
     def y_arrive(k):
+        units = (lax.rem(y + Y - k, Y), lax.rem(y + k, Y))
         for way in range(2):
-            unit = lax.rem(y + (Y - k if way == 0 else k), Y)
-            part = R.at[unit] if k < Y // 2 else R.at[unit, way]
+            part = R.at[units[way]] if k < y_half else R.at[units[way], way]
             remote(part, part, ys.at[way, k], yr.at[way, k], device(y, z, c, x)).wait_recv()
-            if k < Y // 2:
-                y_forward(way, k + 1, unit)
-
-    for way in range(2):
-        y_forward(way, 1, y)
-
-    wide.arrive(1)
+        if k % 2 == 0:
+            y_forward(k, units)
+
+    y_order = [k for pair in tree(y_half) for k in pair]
+    y_forward(0, (y, y))
+
+    todo = wide.events()
+
+    def wide_events(n):
+        for _ in range(min(n, len(todo))):
+            todo.pop(0)()
+
+    wide_events(2)
 
     f_as, f_ar, f_bs, f_br, f_cs, f_cr, f_ds, f_dr = fsems
-    both = jnp.concatenate([gate_rows, up_rows], axis=1)
+    B[...] = jnp.concatenate([gate_rows, up_rows], axis=1).reshape(Z, 16, 2 * ff)
+    order = farthest_first(Z)
+    both = jnp.concatenate([B[lax.rem(z + d, Z)] for d in order], axis=0)
     other = device(y, z, 1 - c, x)
-    for d in range(X):
-        at = pl.multiple_of(((1 - c) * X + d) * CW, CW)
-        FAs[d] = dot(both, wgu[pl.ds(at, CW), :], 1, 1).astype(BF)
+    x_order = farthest_first(X)
+
+    def columns(cc, xx):
+        at = pl.multiple_of((cc * X + xx) * CW, CW)
+        return dot(both, wgu[pl.ds(at, CW), :], 1, 1)
+
+    for d in x_order:
+        FAs[d] = columns(1 - c, lax.rem(x + d, X)).astype(BF)
         go(remote(FAs.at[d], FAr.at[d], f_as.at[d], f_ar.at[d], other))
-    wide.arrive(2)
-    for d in range(X):
-        at = pl.multiple_of((c * X + d) * CW, CW)
-        FO[d] = dot(both, wgu[pl.ds(at, CW), :], 1, 1)
-    wide.arrive(3)
-    for d in range(X):
+    wide_events(1)
+    Zh = Z // 2
+
+    def across(d, g):
+        return FBs.at[d, g], FBr.at[d, g], f_bs.at[d, g], f_br.at[d, g]
+
+    for d in x_order:
+        xx = lax.rem(x + d, X)
+        summed = columns(c, xx)
         remote(FAs.at[d], FAr.at[d], f_as.at[d], f_ar.at[d], other).wait_recv()
-    for d in range(1, X):
-        xx = lax.rem(x + d, X)
-        FBs[d] = (FO[xx] + FAr[xx].astype(F32)).astype(BF)
-        go(remote(FBs.at[d], FBr.at[d], f_bs.at[d], f_br.at[d], device(y, z, c, xx)))
-    for s in range(4, gather.right + 2):
-        wide.arrive(s)
-    total = FO[x] + FAr[x].astype(F32)
-    for d in range(1, X):
-        remote(FBs.at[d], FBr.at[d], f_bs.at[d], f_br.at[d], other).wait_recv()
-        total += FBr[d].astype(F32)
-    FT[...] = total.reshape(Z, 16, CW)
-    FCs[...] = total.astype(BF).reshape(Z, 16, CW)
+        summed += FAr[d].astype(F32)
+        if d:
+            FBs[d] = summed.reshape(2, Zh, 16, CW).astype(BF)
+            go(remote(*across(d, 0), device(y, z, c, xx)))
+        else:
+            FT[...] = summed.reshape(Z, 16, CW)
+    for d in x_order[:-1]:
+        go(remote(*across(d, 1), device(y, z, c, lax.rem(x + d, X))))
+    wide_events(4)
+    for g in range(2):
+        total = FT[g * Zh : (g + 1) * Zh]
+        for d in x_order[:-1]:
+            remote(*across(d, g), other).wait_recv()
+            total += FBr[d, g].astype(F32)
+        FCs[g * Zh : (g + 1) * Zh] = total.astype(BF)
+        for k in range(g * Zh, (g + 1) * Zh):
+            d = order[k]
+            if d:
+                to = device(y, lax.rem(z + d, Z), c, x)
+                go(remote(FCs.at[k], FCr.at[d], f_cs.at[d], f_cr.at[d], to))
+        if g == 1:
+            FT[0] = total[Zh - 1]
+        wide_events(2)
+    y_arrive(y_order[0])
+    wide_events(len(todo))
+    for k in y_order[1:2]:
+        y_arrive(k)
+    total = FT[0]
     for d in range(1, Z):
-        zz = lax.rem(z + d, Z)
-        go(remote(FCs.at[zz], FCr.at[d], f_cs.at[d], f_cr.at[d], device(y, zz, c, x)))
-    if Y > 2:
-        y_arrive(1)
-    total = FT[z]
-    for d in range(1, Z):
-        remote(FCs.at[z], FCr.at[d], f_cs.at[d], f_cr.at[d], other).wait_recv()
+        remote(FCs.at[0], FCr.at[d], f_cs.at[d], f_cr.at[d], other).wait_recv()
         total += FCr[d].astype(F32)
     FDr[mine] = total.astype(BF)
     for d in range(1, 2 * X):
@@ -356,15 +408,13 @@
 
     def accumulate_pair(k):
         accumulate(lax.rem(y + Y - k, Y), False)
-        if k < Y // 2:
+        if k < y_half:
             accumulate(lax.rem(y + k, Y), False)
 
     accumulate(y, True)
-    done = 1
-    for k in range(2, Y // 2):
-        y_arrive(k)
-        accumulate_pair(done)
-        done = k
+    for k in y_order[:2]:
+        if k < y_half:
+            accumulate_pair(k)
 
     for d in range(1, 2 * X):
         j = lax.rem(mine + 2 * X - d, 2 * X)
@@ -379,18 +429,22 @@
     weighted = feature * gain_ref[...]
     along = jnp.mean(weighted * src, axis=-1, keepdims=True)
     grad = weighted * scale - src * (scale * scale * scale * along)
-    grad = jnp.concatenate([grad, jnp.zeros_like(grad)], axis=0).astype(BF)
-    out_b[...] = dot(picks[...], grad).astype(BF)
-
-    while done < Y // 2 - 1:
-        done += 1
-        accumulate_pair(done - 1)
-    if Y > 2:
-        accumulate_pair(done)
-    y_arrive(Y // 2)
-    accumulate_pair(Y // 2)
+    out_s[...] = jnp.concatenate([grad, jnp.zeros_like(grad)], axis=0).astype(BF)
+
+    for k in y_order[2:]:
+        y_arrive(k)
+    for k in y_order:
+        if k in y_order[2:] or k == y_half:
+            accumulate_pair(k)
     for copy in sent:
         copy.wait_send()
+
+
+def results(slots, picks, g_in, u_in, d_in, branch, g_out, u_out, d_out):
+    branch[...] = dot(picks[...], slots[...]).astype(BF)
+    g_out[...] = g_in[...]
+    u_out[...] = u_in[...]
+    d_out[...] = d_in[...]
 
 
 def local(sizes, tokens, cotangent, norm_gain, gate_weight, up_weight, down_weight, depths):
@@ -410,32 +464,35 @@
         dma((2, steps, 2)),
     )
     hbm, whole = pl.BlockSpec(memory_space=pl.ANY), pl.BlockSpec(memory_space=pltpu.VMEM)
-    return pl.pallas_call(
+    grads = (
+        jax.ShapeDtypeStruct((D // Y, ff), F32),
+        jax.ShapeDtypeStruct((D // Y, ff), F32),
+        jax.ShapeDtypeStruct((ff, D // Y), F32),
+    )
+    parts = pl.pallas_call(
         functools.partial(kernel, sizes),
         out_shape=(
-            jax.ShapeDtypeStruct((n_tok // X, D), BF),
-            jax.ShapeDtypeStruct((D // Y, ff), F32),
-            jax.ShapeDtypeStruct((D // Y, ff), F32),
-            jax.ShapeDtypeStruct((ff, D // Y), F32),
+            jax.ShapeDtypeStruct((16, D), BF),
+            jax.ShapeDtypeStruct((n_tok // X, 16), BF),
+            *grads,
         ),
         in_specs=[hbm, hbm, whole, hbm, hbm, hbm, whole],
-        out_specs=(whole,) * 4,
+        out_specs=(whole,) * 5,
         scratch_shapes=[
             vmem((n_tok, D), BF),
             vmem((n_tok, D), BF),
             vmem((D, 2 * ff), BF),
             vmem((ff, D), BF),
             vmem((SLOTS, D), F32),
-            vmem((n_tok // X, 16), BF),
             vmem((Z, 2, 2, 2, 16, QD), BF),
             vmem((Z, 2, 2, 2, Y, 16, HD), BF),
             vmem((Y, 2, 2, 16, HD), BF),
             vmem((Y, 2, 3, N // 2, ff), BF),
             vmem((X, N, CW), BF),
             vmem((X, N, CW), BF),
-            vmem((X, N, CW), F32),
-            vmem((X, N, CW), BF),
-            vmem((X, N, CW), BF),
+            vmem((Z, 16, 2 * ff), BF),
+            vmem((X, 2, Z // 2, 16, CW), BF),
+            vmem((X, 2, Z // 2, 16, CW), BF),
             vmem((Z, 16, CW), F32),
             vmem((Z, 16, CW), BF),
             vmem((Z, 16, CW), BF),
@@ -448,8 +505,8 @@
             (
                 dma((X,)),
                 dma((X,)),
-                dma((X,)),
-                dma((X,)),
+                dma((X, 2)),
+                dma((X, 2)),
                 dma((Z,)),
                 dma((Z,)),
                 dma((2 * X,)),
@@ -468,6 +525,12 @@
         down_weight,
         depths.reshape(1, n_tok),
     )
+    return pl.pallas_call(
+        results,
+        out_shape=(jax.ShapeDtypeStruct((n_tok // X, D), BF), *grads),
+        in_specs=[whole] * 5,
+        out_specs=(whole,) * 4,
+    )(*parts)
 
 
 def solution(mesh):

time: 100 us -> 78.6 us (0.79)
  the two profiles are of different devices: /device:TPU:24 before, /device:TPU:1 now
where the time goes in v2:
time: 78.6 us; the launch traced here: 78.4 us
  Pallas kernels  77.7 us (99%)
    pallas_call x1, Pallas kernels, local(): pl.pallas_call(functools.partial(kernel, sizes), out_shape=(jax.ShapeDtyp...  75.3 us
    pallas_call x1, Pallas kernels, local(): pl.pallas_call(results, out_shape=(jax.ShapeDtypeStruct((n_tok // X, D),...  2.44 us

profile of v2, /device:TPU:1, one launch (start us, length us, event | category | flops | bytes accessed | tf_op | source)
XLA Modules:
  0.0 78.4 jit_solution(10088597049132667365)
XLA Ops:
  0.6 75.3 %shard_map.102 = (bf16[16,4096]{1,0:T(8,128)(2,1)}, bf16[64,16]{1,0:T(8,128)(2,1)}, f32[512,128]{1,0:T(8,128)}, f32[512,128]{1,0:T(8,128)}, f32[128,512]{1,0:T(8,128)}) custom-call(bf16[256,4096]{1,0:T(8,128)(2,1)} %tok_hbm.1, bf16[256,4096]{1,0:T(8,128)(2,1)} %cot_hbm.1, f32[1,4096]{1,0:T(1,128)} %bitcast.2, bf16[4096,128]{1,0:T(8,128)(2,1)} %gw_hbm.1, ...), custom_call_target="tpu_custom_call" | custom-call | tf_op jit(solution)/shard_map/pallas_call | solution.py:472
  75.9 2.4 %shard_map.103 = (bf16[64,4096]{1,0:T(8,128)(2,1)}, f32[512,128]{1,0:T(8,128)}, f32[512,128]{1,0:T(8,128)}, f32[128,512]{1,0:T(8,128)}) custom-call(bf16[16,4096]{1,0:T(8,128)(2,1)} %get-tuple-element.9.slots, bf16[64,16]{1,0:T(8,128)(2,1)} %get-tuple-element.10.picks, f32[512,128]{1,0:T(8,128)} %get-tuple-element.11.g_in, ...), custom_call_target="tpu_custom_call" | custom-call | tf_op jit(solution)/shard_map/pallas_call | solution.py:528

commit v3 on v2

--- a/solution.py
+++ b/solution.py
@@ -51,8 +51,11 @@
 
     def events(self):
         found = []
+        self.last_forward = None
         for k, group in enumerate(self.groups):
             found.append(functools.partial(self.arrive, group[0]))
+            if k + 1 < len(self.groups):
+                self.last_forward = found[-1]
             if k:
                 found += [functools.partial(self.beside, s) for s in self.groups[k - 1]]
             found += [functools.partial(self.arrive, s) for s in group[1:]]
@@ -236,9 +239,6 @@
             for q in range(2):
                 at = (yy * 4 + h * 2 + q) * HD
                 S[yy, h, q] = block[:, at : at + HD]
-    for h in range(2):
-        for q in range(2):
-            H[z, c, h, q, y] = S[y, h, q]
 
     pl.semaphore_wait(barrier, len(partners))
 
@@ -256,18 +256,28 @@
         yy = lax.rem(y + d, Y)
         go(
             remote(
-                S.at[yy], H.at[z, c, :, :, y], as_.at[d], ar.at[d], device(yy, z, c, x)
+                S.at[yy], H.at[z, c, :, :, Y - 1 - d], as_.at[d], ar.at[d], device(yy, z, c, x)
             )
         )
-    for event in gather.events():
+    wide = PlaneGather(H, hsems, where, sizes, device, sent)
+    events = gather.events()
+    behind = events.index(gather.last_forward) + 1 if gather.last_forward else 0
+    for event in events[:behind]:
         event()
     for d in range(1, Y):
-        yy = lax.rem(y + Y - d, Y)
-        part = H.at[z, c, :, :, yy]
-        remote(S.at[yy], part, as_.at[d], ar.at[d], device(y, z, c, x)).wait_recv()
-    wide = PlaneGather(H, hsems, where, sizes, device, sent)
+        part = H.at[z, c, :, :, Y - 1 - d]
+        remote(S.at[y], part, as_.at[d], ar.at[d], device(y, z, c, x)).wait_recv()
     wide.start()
+    for event in events[behind:]:
+        event()
     gather.finish()
+    todo = wide.events()
+
+    def wide_events(n):
+        for _ in range(min(n, len(todo))):
+            todo.pop(0)()
+
+    wide_events(1)
 
     for load in loads[2:]:
         load.wait()
@@ -316,13 +326,7 @@
     y_order = [k for pair in tree(y_half) for k in pair]
     y_forward(0, (y, y))
 
-    todo = wide.events()
-
-    def wide_events(n):
-        for _ in range(min(n, len(todo))):
-            todo.pop(0)()
-
-    wide_events(2)
+    wide_events(1)
 
     f_as, f_ar, f_bs, f_br, f_cs, f_cr, f_ds, f_dr = fsems
     B[...] = jnp.concatenate([gate_rows, up_rows], axis=1).reshape(Z, 16, 2 * ff)
@@ -356,7 +360,7 @@
             FT[...] = summed.reshape(Z, 16, CW)
     for d in x_order[:-1]:
         go(remote(*across(d, 1), device(y, z, c, lax.rem(x + d, X))))
-    wide_events(4)
+    wide_events(3)
     for g in range(2):
         total = FT[g * Zh : (g + 1) * Zh]
         for d in x_order[:-1]:
@@ -370,9 +374,8 @@
                 go(remote(FCs.at[k], FCr.at[d], f_cs.at[d], f_cr.at[d], to))
         if g == 1:
             FT[0] = total[Zh - 1]
-        wide_events(2)
+        wide_events((1, 3)[g])
     y_arrive(y_order[0])
-    wide_events(len(todo))
     for k in y_order[1:2]:
         y_arrive(k)
     total = FT[0]
@@ -382,9 +385,17 @@
     FDr[mine] = total.astype(BF)
     for d in range(1, 2 * X):
         go(remote(FDr.at[mine], FDr.at[mine], f_ds.at[d], f_dr.at[d], corner(d)))
-    wide.finish()
-
-    def accumulate(unit, first):
+
+    at_own = y * (4 * HD)
+    own_h, own_q = at_own // (2 * QD), lax.rem(at_own // QD, 2)
+
+    def block_of(slot, h, q):
+        if slot is not None:
+            return H[:, :, h, q, slot]
+        at = pl.multiple_of(lax.rem(at_own, QD) + (h * 2 + q) * HD, HD)
+        return G[:, :, own_h, own_q, :, pl.ds(at, HD)]
+
+    def accumulate(unit, slot=None):
         rows_g = jnp.concatenate([R[unit, 0, 0], R[unit, 1, 0]], axis=0)
         rows_u = jnp.concatenate([R[unit, 0, 1], R[unit, 1, 1]], axis=0)
         rows_h = jnp.concatenate([R[unit, 0, 2], R[unit, 1, 2]], axis=0)
@@ -392,12 +403,12 @@
         for h in range(2):
             for q in range(2):
                 at = (h * 2 + q) * HD
-                a = H[:, :, h, q, unit].astype(F32).reshape(Z * 2, 2, SLOTS, HD)
+                a = block_of(slot, h, q).astype(F32).reshape(Z * 2, 2, SLOTS, HD)
                 nrm = a[:, 0].reshape(N, HD).astype(BF)
                 msk = a[:, 1].reshape(N, HD).astype(BF)
                 pair = dot(nrm, gu_rows, 0, 0)
                 down = dot(rows_h, msk, 0, 0)
-                if first:
+                if slot is None:
                     out_g[at : at + HD, :] = pair[:, :ff]
                     out_u[at : at + HD, :] = pair[:, ff:]
                     out_d[:, at : at + HD] = down
@@ -407,11 +418,13 @@
                     out_d[:, at : at + HD] += down
 
     def accumulate_pair(k):
-        accumulate(lax.rem(y + Y - k, Y), False)
+        accumulate(lax.rem(y + Y - k, Y), Y - 1 - k)
         if k < y_half:
-            accumulate(lax.rem(y + k, Y), False)
-
-    accumulate(y, True)
+            accumulate(lax.rem(y + k, Y), k - 1)
+
+    wide_events(len(todo))
+    wide.finish()
+    accumulate(y)
     for k in y_order[:2]:
         if k < y_half:
             accumulate_pair(k)
@@ -485,7 +498,7 @@
             vmem((ff, D), BF),
             vmem((SLOTS, D), F32),
             vmem((Z, 2, 2, 2, 16, QD), BF),
-            vmem((Z, 2, 2, 2, Y, 16, HD), BF),
+            vmem((Z, 2, 2, 2, Y - 1, 16, HD), BF),
             vmem((Y, 2, 2, 16, HD), BF),
             vmem((Y, 2, 3, N // 2, ff), BF),
             vmem((X, N, CW), BF),

time: 78.6 us -> 75.7 us (0.963)
  Pallas kernels: 77.7 us -> 74.9 us
    pallas_call x1, Pallas kernels: 75.3 us -> 72.4 us  [local(): pl.pallas_call(functools.partial(kernel, sizes), out_shape=(jax.ShapeDtyp...]
where the time goes in v3:
time: 75.7 us; the launch traced here: 75.5 us
  Pallas kernels  74.9 us (99%)
    pallas_call x1, Pallas kernels, local(): pl.pallas_call(functools.partial(kernel, sizes), out_shape=(jax.ShapeDtyp...  72.4 us
    pallas_call x1, Pallas kernels, local(): pl.pallas_call(results, out_shape=(jax.ShapeDtypeStruct((n_tok // X, D),...  2.44 us

profile of v3, /device:TPU:1, one launch (start us, length us, event | category | flops | bytes accessed | tf_op | source)
XLA Modules:
  0.0 75.5 jit_solution(8517585066884862901)
XLA Ops:
  0.6 72.4 %shard_map.102 = (bf16[16,4096]{1,0:T(8,128)(2,1)}, bf16[64,16]{1,0:T(8,128)(2,1)}, f32[512,128]{1,0:T(8,128)}, f32[512,128]{1,0:T(8,128)}, f32[128,512]{1,0:T(8,128)}) custom-call(bf16[256,4096]{1,0:T(8,128)(2,1)} %tok_hbm.1, bf16[256,4096]{1,0:T(8,128)(2,1)} %cot_hbm.1, f32[1,4096]{1,0:T(1,128)} %bitcast.2, bf16[4096,128]{1,0:T(8,128)(2,1)} %gw_hbm.1, ...), custom_call_target="tpu_custom_call" | custom-call | tf_op jit(solution)/shard_map/pallas_call | solution.py:485
  73.1 2.4 %shard_map.103 = (bf16[64,4096]{1,0:T(8,128)(2,1)}, f32[512,128]{1,0:T(8,128)}, f32[512,128]{1,0:T(8,128)}, f32[128,512]{1,0:T(8,128)}) custom-call(bf16[16,4096]{1,0:T(8,128)(2,1)} %get-tuple-element.9.slots, bf16[64,16]{1,0:T(8,128)(2,1)} %get-tuple-element.10.picks, f32[512,128]{1,0:T(8,128)} %get-tuple-element.11.g_in, ...), custom_call_target="tpu_custom_call" | custom-call | tf_op jit(solution)/shard_map/pallas_call | solution.py:541
